TPU v7x, 32 devices: a whole 2x2x4 slice. The times are simulated.
32 devices in a mesh: lat: 8 (over y, x, core), lon: 4 (over z).
Axes of the slice: x: 2, y: 2, z: 4, core: 2. Of those that a mesh axis runs over, the one named last changes fastest.
Arguments:
- current_sample: float32 [4, 256, 1024], P(None, 'lat', 'lon'), may hold values from -6 to 6
- churn_noise: float32 [4, 256, 1024], P(None, 'lat', 'lon'), may hold values from -6 to 6
- coarse_fields: float32 [12, 32, 128], P(None, 'lat', 'lon'), may hold values from -6 to 6
- tile_owner: int32 [8], replicated, may hold values from 0 to 7, each once
- input_kernel: bfloat16 [3, 3, 16, 128], replicated, may hold values from -0.5 to 0.5
- fine_first: bfloat16 [3, 3, 128, 128], replicated, may hold values from -0.1875 to 0.1875
- fine_second: bfloat16 [3, 3, 128, 128], replicated, may hold values from -0.1875 to 0.1875
- coarse_first: bfloat16 [3, 3, 128, 128], replicated, may hold values from -0.1875 to 0.1875
- coarse_second: bfloat16 [3, 3, 128, 128], replicated, may hold values from -0.1875 to 0.1875
- output_kernel: bfloat16 [3, 3, 128, 4], replicated, may hold values from -0.5 to 0.5
Outputs:
- next_sample: float32 [4, 256, 1024], P(None, 'lat', 'lon')
Inputs may be any that keep to these rules, and one draw needn't show every extreme that they name: `tile_owner`: each value is the row block's position along the bands; every stored block covers exactly one band.
All inputs are finite; a program needn't handle non-finite values.
Results may differ from a plain program's by a relative error of at most 0.0055.
Values may be sent and summed in bfloat16 or wider, within the bound.
A program may use at most 64 MiB of HBM per device.

v0:
```python
import functools
import math

import jax
import jax.numpy as jnp
from jax import lax
from jax.experimental import pallas as pl
from jax.experimental.pallas import tpu as pltpu
from jax.sharding import PartitionSpec as P

RATIO = 8
Q = 16
COL_HALO = 16
OUT_HALO = 6
ROW_HALO = OUT_HALO + 3
CELL_HALO = 2

sigma_now = 1.0
sigma_hat = 1.2
sigma_next = 0.4
sigma_data = 0.5
half_root = math.sqrt(0.5)
f32 = jnp.float32
bf16 = jnp.bfloat16


def silu(v):
    h = 0.5 * v
    return h + h * jnp.tanh(h)


def put_row(ref, row, value, span):
    channels = value.shape[-1]
    value = value.reshape(span, Q, channels)
    ref[row, pl.ds(1, span)] = value.astype(bf16)
    ref[row, 0] = pltpu.roll(value[span - 1], 1, 0).astype(bf16)
    ref[row, span + 1] = pltpu.roll(value[0], Q - 1, 0).astype(bf16)


def conv_pair(src, row, forward, weights, span):
    channels = src.shape[-1]
    parts = []
    for k in range(4):
        at = jnp.where(forward, row + k, row + 3 - k)
        for b in range(3):
            parts.append(src[at, pl.ds(b, span)].reshape(span * Q, channels))
    return jnp.dot(jnp.concatenate(parts, axis=1), weights[...], preferred_element_type=f32)


def kernel(
    north, south, halves_ref, ext_ref, cell_ref, pert_ref, stem_w, first_w, second_w, cfirst_w, csecond_w, out_w,
    res_ref, net, stem, act, hidden, fine, pooled, cact, chidden, cout, terms, rows_out,
):
    del halves_ref
    variables, rows, width = pert_ref.shape
    channels = stem.shape[-1]
    span = stem.shape[1]
    half_span = span // 2
    pixels = span * Q
    lanes = net.shape[-1]
    ext_cols = ext_ref.shape[1]
    ext_rows = rows + 2 * ROW_HALO

    def onehot(depth, cell):
        at = lax.broadcasted_iota(jnp.int32, (depth, lanes), 0)
        lane = lax.broadcasted_iota(jnp.int32, (depth, lanes), 1)
        column = (lane % Q) * span + lane // Q - 1
        inside = (column >= 0) & (column < ext_cols) & (lane < (span + 2) * Q)
        return jnp.where(inside & (at == column // cell), 1.0, 0.0).astype(bf16)

    fine_cols = jnp.dot(ext_ref[...], onehot(ext_cols, 1), preferred_element_type=f32)
    cell_cols = jnp.dot(cell_ref[...], onehot(cell_ref.shape[1], RATIO), preferred_element_type=f32)
    for r in range(ext_rows):
        cell = (r - ROW_HALO + CELL_HALO * RATIO) // RATIO
        both = fine_cols[r * 16 : r * 16 + 16] + cell_cols[cell * 16 : cell * 16 + 16]
        for b in range(3):
            moved = both if b == 0 else pltpu.roll(both, lanes - b * Q, 1)
            net[r, pl.ds(b * 16, 16)] = moved.astype(bf16)

    def regions(halo_pairs, pairs, body):
        def step(i, carry):
            mirrored = (north & (i < halo_pairs)) | (south & (i >= halo_pairs + pairs))
            body(i, jnp.logical_not(mirrored))
            return carry

        lax.fori_loop(0, 2 * halo_pairs + pairs, step, 0)

    def order(row, forward):
        return jnp.where(forward, row, row + 1), jnp.where(forward, row + 1, row)

    stem_halo = ROW_HALO - 1

    def stem_step(i, forward):
        parts = [net[jnp.where(forward, 2 * i + k, 2 * i + 3 - k)][:, :pixels] for k in range(4)]
        both = lax.dot_general(
            jnp.concatenate(parts, axis=0), stem_w[...], (((0,), (0,)), ((), ())), preferred_element_type=f32
        )
        for p, at in enumerate(order(2 * i, forward)):
            value = both[:, p * channels : (p + 1) * channels].astype(bf16)
            stem[at] = value.reshape(span, Q, channels)
            put_row(act, at + 1, silu(value.astype(f32)), span)

    act[0] = jnp.zeros(act.shape[1:], bf16)
    act[ext_rows - 1] = jnp.zeros(act.shape[1:], bf16)
    regions(stem_halo // 2, rows // 2, stem_step)

    def first_step(i, forward):
        both = conv_pair(act, 2 * i, forward, first_w, span)
        for p, at in enumerate(order(2 * i, forward)):
            put_row(hidden, at, silu(both[:, p * channels : (p + 1) * channels]), span)

    regions(stem_halo // 2, rows // 2, first_step)

    def second_step(i, forward):
        both = conv_pair(hidden, 2 * i + 1, forward, second_w, span)
        total = jnp.zeros((half_span, Q, channels), f32)
        for p, at in enumerate(order(2 * i, forward)):
            value = both[:, p * channels : (p + 1) * channels].reshape(span, Q, channels)
            value = ((stem[at + 2].astype(f32) + value) * half_root).astype(bf16)
            fine[at] = value
            split = value.astype(f32).reshape(half_span, 2, Q, channels)
            total = total + (split[:, 0] + split[:, 1])
        mean = (total * 0.25).astype(bf16)
        pooled[i] = mean
        put_row(cact, i, silu(mean.astype(f32)).reshape(half_span * Q, channels), half_span)

    regions(OUT_HALO // 2, rows // 2, second_step)
    chidden[0] = jnp.zeros(chidden.shape[1:], bf16)
    chidden[chidden.shape[0] - 1] = jnp.zeros(chidden.shape[1:], bf16)

    def cfirst_step(i, forward):
        both = conv_pair(cact, 2 * i, forward, cfirst_w, half_span)
        for p, at in enumerate(order(2 * i, forward)):
            put_row(chidden, at + 1, silu(both[:, p * channels : (p + 1) * channels]), half_span)

    regions(1, rows // 4, cfirst_step)

    def csecond_step(i, forward):
        both = conv_pair(chidden, 2 * i, forward, csecond_w, half_span)
        for p, at in enumerate(order(2 * i, forward)):
            value = both[:, p * channels : (p + 1) * channels].reshape(half_span, Q, channels)
            cout[at] = ((pooled[at + 1].astype(f32) + value) * half_root).astype(bf16)

    regions(1, rows // 4, csecond_step)

    def merge_step(r, carry):
        wide = cout[(r + 3) // 2].astype(f32)[:, None]
        value = fine[r + OUT_HALO - 1].astype(f32).reshape(half_span, 2, Q, channels)
        value = silu((value + wide) * half_root).reshape(span, Q, channels)
        before = pltpu.roll(value[span - 1], 1, 0)[None]
        after = pltpu.roll(value[0], Q - 1, 0)[None]
        value = jnp.concatenate([before, value, after], axis=0).astype(bf16)
        terms[r] = lax.dot_general(
            out_w[...],
            value.reshape((span + 2) * Q, channels),
            (((1,), (1,)), ((), ())),
            preferred_element_type=f32,
        )
        return carry

    lax.fori_loop(0, rows + 2, merge_step, 0)

    def gather_step(r, carry):
        total = None
        for b in range(3):
            part = terms[r, pl.ds(8 * b, 8)]
            for a in range(1, 3):
                part = part + terms[r + a, pl.ds(8 * (3 * a + b), 8)]
            part = part[:, b * Q : b * Q + pixels]
            total = part if total is None else total + part
        rows_out[r] = total
        return carry

    lax.fori_loop(0, rows, gather_step, 0)

    lane = lax.broadcasted_iota(jnp.int32, (pixels, width), 0)
    column = lax.broadcasted_iota(jnp.int32, (pixels, width), 1)
    back = jnp.where((lane % Q) * span + lane // Q == column + COL_HALO, 1.0, 0.0).astype(bf16)
    permuted = rows_out[...].reshape(rows * 8, pixels)
    high = permuted.astype(bf16)
    rest = permuted - high.astype(f32)
    middle = rest.astype(bf16)
    low = (rest - middle.astype(f32)).astype(bf16)
    network = jnp.dot(high, back, preferred_element_type=f32)
    network = network + jnp.dot(middle, back, preferred_element_type=f32)
    network = network + jnp.dot(low, back, preferred_element_type=f32)
    network = jnp.swapaxes(network.reshape(rows, 8, width), 0, 1)[:variables]
    perturbed = pert_ref[...]
    denom = sigma_hat**2 + sigma_data**2
    denoised = sigma_data**2 / denom * perturbed + sigma_hat * sigma_data / math.sqrt(denom) * network
    res_ref[...] = perturbed + (sigma_next - sigma_hat) / sigma_hat * (perturbed - denoised)


def entry(bands, refs):
    band = lax.axis_index("lat")
    kernel(band == 0, band == bands - 1, None, *refs)


def pair_weights(taps):
    low = jnp.pad(taps, ((0, 1), (0, 0), (0, 0), (0, 0)))
    high = jnp.pad(taps, ((1, 0), (0, 0), (0, 0), (0, 0)))
    both = jnp.concatenate([low, high], axis=3)
    return both.reshape(-1, both.shape[3])


def rows_with_halo(own, above, below, across_first, across_last):
    band = lax.axis_index("lat")
    bands = lax.axis_size("lat")
    north = jnp.where(band == 0, jnp.flip(across_first, 1), above)
    south = jnp.where(band == bands - 1, jnp.flip(across_last, 1), below)
    return jnp.concatenate([north, own, south], axis=1)


def across_pole(own, halo):
    sectors = lax.axis_size("lon")
    edges = jnp.concatenate([own[:, :halo], own[:, -halo:]], axis=1)
    got = lax.ppermute(edges, "lon", [(i, (i + sectors // 2) % sectors) for i in range(sectors)])
    return got[:, :halo], got[:, halo:]


def columns_with_halo(own, halo):
    sectors = lax.axis_size("lon")
    up = [(i, (i + 1) % sectors) for i in range(sectors)]
    before = lax.ppermute(own[:, :, -halo:], "lon", up)
    after = lax.ppermute(own[:, :, :halo], "lon", [(j, i) for i, j in up])
    return jnp.concatenate([before, own, after], axis=2)


def body(
    current_sample,
    churn_noise,
    coarse_fields,
    tile_owner,
    input_kernel,
    fine_first,
    fine_second,
    coarse_first,
    coarse_second,
    output_kernel,
):
    band = lax.axis_index("lat")
    bands = lax.axis_size("lat")
    variables, rows, width = current_sample.shape
    channels = fine_first.shape[3]
    span = (width + 2 * COL_HALO) // Q
    pixels = span * Q
    ext_rows = rows + 2 * ROW_HALO
    ins = input_kernel.shape[2]

    perturbed = current_sample + math.sqrt(sigma_hat**2 - sigma_now**2) * churn_noise
    scale_in = 1.0 / math.sqrt(sigma_hat**2 + sigma_data**2)
    noisy = (perturbed * scale_in).astype(bf16)
    up = [(i, i + 1) for i in range(bands - 1)]
    down = [(j, i) for i, j in up]
    above = lax.ppermute(noisy[:, -ROW_HALO:], "lat", up)
    below = lax.ppermute(noisy[:, :ROW_HALO], "lat", down)
    ext = columns_with_halo(rows_with_halo(noisy, above, below, *across_pole(noisy, ROW_HALO)), COL_HALO)

    block_rows = coarse_fields.shape[1]
    gathered = lax.all_gather(coarse_fields.astype(bf16), "lat", axis=1, tiled=True)

    def tile(which):
        slot = tile_owner[jnp.clip(which, 0, bands - 1)]
        return lax.dynamic_slice_in_dim(gathered, slot * block_rows, block_rows, 1)

    own = tile(band)
    cells = rows_with_halo(
        own, tile(band - 1)[:, -CELL_HALO:], tile(band + 1)[:, :CELL_HALO], *across_pole(own, CELL_HALO)
    )
    cells = columns_with_halo(cells, COL_HALO // RATIO)

    ext = jnp.pad(ext.transpose(1, 0, 2), ((0, 0), (0, ins - variables), (0, 0))).reshape(ext_rows * ins, -1)
    cells = cells.transpose(1, 0, 2)
    cells = jnp.pad(cells, ((0, 0), (variables, 0), (0, 128 - cells.shape[2])))
    cells = cells.reshape(-1, 128)
    out_w = jnp.pad(jnp.transpose(output_kernel, (0, 1, 3, 2)), ((0, 0), (0, 0), (0, 8 - variables), (0, 0)))
    out_w = out_w.reshape(-1, channels)

    lanes = -(-(span + 2) * Q // 128) * 128
    half_span = span // 2
    field = lambda n, s: pltpu.VMEM((n, s, Q, channels), bf16)
    fine_rows = rows + 2 * OUT_HALO
    vmem = pl.BlockSpec(memory_space=pltpu.VMEM)

    def call(*refs):
        entry(bands, refs)

    return pl.pallas_call(
        call,
        out_shape=jax.ShapeDtypeStruct(current_sample.shape, f32),
        in_specs=[vmem] * 9,
        out_specs=vmem,
        scratch_shapes=[
            pltpu.VMEM((ext_rows, 3 * ins, lanes), bf16),
            field(ext_rows - 2, span),
            field(ext_rows, span + 2),
            field(ext_rows - 2, span + 2),
            field(fine_rows, span),
            field(fine_rows // 2, half_span),
            field(fine_rows // 2, half_span + 2),
            field(fine_rows // 2, half_span + 2),
            field(fine_rows // 2 - 2, half_span),
            pltpu.VMEM((rows + 2, out_w.shape[0], (span + 2) * Q), f32),
            pltpu.VMEM((rows, 8, pixels), f32),
        ],
        compiler_params=pltpu.CompilerParams(vmem_limit_bytes=56 << 20),
    )(
        ext,
        cells,
        perturbed,
        pair_weights(input_kernel),
        pair_weights(fine_first),
        pair_weights(fine_second),
        pair_weights(coarse_first),
        pair_weights(coarse_second),
        out_w,
    )


def solution(mesh):
    placed = (P(None, "lat", "lon"),) * 3 + (P(),) * 7
    return jax.shard_map(
        body, mesh=mesh, in_specs=placed, out_specs=P(None, "lat", "lon"), check_vma=False
    )
```

profile of v0, /device:TPU:0, one launch (start us, length us, event | category | flops | bytes accessed | tf_op | source)
XLA Modules:
  0.0 86.3 jit_solution(5898117135325267990)
XLA Ops:
  0.0 0.0 copy-start
  0.0 1.4 %fusion.20 = (s32[1]{0:T(128)}, s32[1]{0:T(128)}, s32[1]{0:T(128)}) fusion(s32[8]{0:T(128)} %param.13, s32[]{:T(128)S(6)} %min.11, s32[]{:T(128)S(6)} %min.10, s32[]{:T(128)S(6)} %min.12), kind=kLoop, calls=%fused_computation.36 | loop fusion | bytes 36 | tf_op jit(solution)/shard_map/dynamic_slice | solution.py:263
  2.1 0.7 convert_element_type.27
  2.8 10.7 %all_gather.3 = bf16[12,32,32]{2,0,1:T(8,128)(2,1)S(1)} all-gather(bf16[12,4,32]{2,0,1:T(8,128)(2,1)S(1)} %copy.17), channel_id=1, replica_groups=mesh['lat'=8,'lon'=4] {'lat'}, dimensions={1}, use_global_device_ids=true | all-gather | bytes 27648 | tf_op jit(solution)/shard_map/all_gather | solution.py:260
  13.5 0.0 copy-start.1
  13.5 2.6 %collective-permute-start.5 = (bf16[12,4,32]{2,0,1:T(8,128)(2,1)S(1)}, bf16[12,4,32]{2,0,1:T(8,128)(2,1)S(1)}, u32[]{:S(2)}, u32[]{:S(2)}) collective-permute-start(bf16[12,4,32]{2,0,1:T(8,128)(2,1)S(1)} %constant_dynamic-slice_fusion), channel_id=1, source_target_pairs={{0,2},{1,3},{2,0},{3,1},{4,6},{5,7},{6,4},{7,5},{8,10},{9,11},{10,... | collective-permute-start | bytes 9224 | tf_op jit(solution)/shard_map/ppermute | solution.py:217
  16.1 1.6 %multiply_convert_fusion = (bf16[4,32,256]{2,1,0:T(8,128)(2,1)S(1)}, f32[4,32,256]{2,1,0:T(8,128)}) fusion(f32[4,32,256]{2,1,0:T(8,128)} %param.10, f32[4,32,256]{2,1,0:T(8,128)} %param.11), kind=kLoop, calls=%fused_computation.19 | loop fusion | flops 131072 | bytes 458752 | tf_op jit(solution)/shard_map/convert_element_type | solution.py:252
  17.7 1.3 %collective-permute-start.2 = (bf16[4,9,256]{2,1,0:T(8,128)(2,1)S(1)}, bf16[4,9,256]{2,1,0:T(8,128)(2,1)S(1)}, u32[]{:S(2)}, u32[]{:S(2)}) collective-permute-start(bf16[4,9,256]{2,1,0:T(8,128)(2,1)S(1)} %get-tuple-element.11), channel_id=1, source_target_pairs={{4,0},{8,4},{12,8},{16,12},{20,16},{24,20},{28,24},{5,1},{9,5},{13... | collective-permute-start | bytes 55304 | tf_op jit(solution)/shard_map/ppermute | solution.py:256
  19.0 3.0 %collective-permute-start.1 = (bf16[4,9,256]{2,1,0:T(8,128)(2,1)S(1)}, bf16[4,9,256]{2,1,0:T(8,128)(2,1)S(1)}, u32[]{:S(2)}, u32[]{:S(2)}) collective-permute-start(bf16[4,9,256]{2,1,0:T(8,128)(2,1)S(1)} %get-tuple-element.12), channel_id=1, source_target_pairs={{0,4},{4,8},{8,12},{12,16},{16,20},{20,24},{24,28},{1,5},{5,9},{9,... | collective-permute-start | bytes 55304 | tf_op jit(solution)/shard_map/ppermute | solution.py:255
  22.1 0.4 collective-permute-start
  22.5 0.0 copy-done
  22.5 0.9 %fusion.8 = bf16[4,3,128,256]{3,2,1,0:T(8,128)(2,1)} fusion(bf16[3,3,128,128]{3,2,1,0:T(8,128)(2,1)S(1)} %copy-done), kind=kLoop, calls=%fused_computation.10 | loop fusion | flops 3145728 | bytes 1081344 | tf_op jit(solution)/shard_map/concatenate | solution.py:202
  23.5 0.0 copy-done.1
  23.5 0.0 copy-start.2
  23.5 1.0 %fusion.9 = bf16[4,3,128,256]{3,2,1,0:T(8,128)(2,1)} fusion(bf16[3,3,128,128]{3,2,1,0:T(8,128)(2,1)S(1)} %copy-done.1), kind=kLoop, calls=%fused_computation.11 | loop fusion | flops 3145728 | bytes 1081344 | tf_op jit(solution)/shard_map/concatenate | solution.py:202
  24.4 0.0 copy-done.2
  24.4 0.0 copy-start.3
  24.4 0.9 %fusion.10 = bf16[4,3,128,256]{3,2,1,0:T(8,128)(2,1)} fusion(bf16[3,3,128,128]{3,2,1,0:T(8,128)(2,1)S(1)} %copy-done.2), kind=kLoop, calls=%fused_computation.12 | loop fusion | flops 3145728 | bytes 1081344 | tf_op jit(solution)/shard_map/concatenate | solution.py:202
  25.4 0.0 copy-done.3
  25.4 0.0 copy-start.4
  25.4 0.0 copy-start.5
  25.4 1.0 %fusion.11 = bf16[4,3,128,256]{3,2,1,0:T(8,128)(2,1)} fusion(bf16[3,3,128,128]{3,2,1,0:T(8,128)(2,1)S(1)} %copy-done.3), kind=kLoop, calls=%fused_computation.13 | loop fusion | flops 3145728 | bytes 1081344 | tf_op jit(solution)/shard_map/concatenate | solution.py:202
  26.4 0.0 copy-done.4
  26.4 0.6 fusion.14
  28.3 0.0 copy-done.5
  28.3 0.6 pad.58
  28.9 0.0 collective-permute-done.5
  29.0 0.1 fusion.18
  29.1 1.6 %collective-permute-start.6 = (bf16[12,8,2]{2,0,1:T(8,128)(2,1)S(1)}, bf16[12,8,2]{2,0,1:T(8,128)(2,1)S(1)}, u32[]{:S(2)}, u32[]{:S(2)}) collective-permute-start(bf16[12,8,2]{2,0,1:T(8,128)(2,1)S(1)} %get-tuple-element.15), channel_id=1, source_target_pairs={{0,1},{1,2},{2,3},{3,0},{4,5},{5,6},{6,7},{7,4},{8,9},{9,10},{10,1... | collective-permute-start | bytes 1160 | tf_op jit(solution)/shard_map/ppermute | solution.py:224
  30.7 2.2 %collective-permute-start.7 = (bf16[12,8,2]{2,0,1:T(8,128)(2,1)S(1)}, bf16[12,8,2]{2,0,1:T(8,128)(2,1)S(1)}, u32[]{:S(2)}, u32[]{:S(2)}) collective-permute-start(bf16[12,8,2]{2,0,1:T(8,128)(2,1)S(1)} %get-tuple-element.16), channel_id=1, source_target_pairs={{1,0},{2,1},{3,2},{0,3},{5,4},{6,5},{7,6},{4,7},{9,8},{10,9},{11,1... | collective-permute-start | bytes 1160 | tf_op jit(solution)/shard_map/ppermute | solution.py:225
  32.9 0.0 collective-permute-done
  33.0 0.1 rev.14
  33.1 0.0 collective-permute-done.1
  33.1 0.1 rev.15
  33.2 0.0 collective-permute-done.2
  33.3 0.1 fusion.15
  33.4 0.1 collective-permute-start.3
  33.5 3.8 %collective-permute-start.4 = (bf16[4,50,16]{2,1,0:T(8,128)(2,1)S(1)}, bf16[4,50,16]{2,1,0:T(8,128)(2,1)S(1)}, u32[]{:S(2)}, u32[]{:S(2)}) collective-permute-start(bf16[4,50,16]{2,1,0:T(8,128)(2,1)S(1)} %get-tuple-element.10), channel_id=1, source_target_pairs={{1,0},{2,1},{3,2},{0,3},{5,4},{6,5},{7,6},{4,7},{9,8},{10,9},{11,1... | collective-permute-start | bytes 19208 | tf_op jit(solution)/shard_map/ppermute | solution.py:225
  37.3 0.0 collective-permute-done.6
  37.3 0.0 collective-permute-done.7
  37.3 0.1 maximum_bitcast_fusion.1
  37.4 0.6 pad.47
  38.0 2.0 %collective-permute-done.3 = bf16[4,50,16]{2,1,0:T(8,128)(2,1)S(1)} collective-permute-done((bf16[4,50,16]{2,1,0:T(8,128)(2,1)S(1)}, bf16[4,50,16]{2,1,0:T(8,128)(2,1)S(1)}, u32[]{:S(2)}, u32[]{:S(2)}) %collective-permute-start.3) | collective-permute-done | bytes 6432 | tf_op jit(solution)/shard_map/ppermute | solution.py:224
  40.0 0.0 collective-permute-done.4
  40.0 0.2 maximum_bitcast_fusion
  40.2 0.1 copy.18
  40.3 0.9 %pad.46.clone = bf16[50,16,288]{2,1,0:T(8,128)(2,1)} pad(bf16[50,4,288]{2,1,0:T(4,128)(2,1)S(1)} %copy.18, bf16[]{:T(256)} %constant.26.clone.1), padding=0_0x0_12x0_0 | pad | bytes 576002 | tf_op jit(solution)/shard_map/jit(_pad)/pad | solution.py:272
  41.2 45.1 %shard_map.100 = f32[4,32,256]{2,1,0:T(8,128)} custom-call(bf16[800,288]{1,0:T(8,128)(2,1)} %bitcast.20, bf16[128,128]{1,0:T(8,128)(2,1)} %bitcast.22, f32[4,32,256]{2,1,0:T(8,128)} %get-tuple-element.6.refs_2_, bf16[192,256]{1,0:T(8,128)(2,1)} %bitcast.21, bf16[1536,256]{1,0:T(8,128)(2,1)} %bitcast.16, bf16[1536,256]{1,0:T(8,128)(2,1)} %bitcast.17, ...), custom_call_target="tpu_custom_call" | custom-call | tf_op jit(solution)/shard_map/pallas_call | solution.py:288
  (11 shorter events, 0.1 us)
Async XLA Ops:
  0.0 22.5 %copy-start = (bf16[3,3,128,128]{3,2,1,0:T(8,128)(2,1)S(1)}, bf16[3,3,128,128]{3,2,1,0:T(8,128)(2,1)}, u32[]{:S(2)}) copy-start(bf16[3,3,128,128]{3,2,1,0:T(8,128)(2,1)} %param.15) | copy-start | bytes 884740
  13.5 10.0 %copy-start.1 = (bf16[3,3,128,128]{3,2,1,0:T(8,128)(2,1)S(1)}, bf16[3,3,128,128]{3,2,1,0:T(8,128)(2,1)}, u32[]{:S(2)}) copy-start(bf16[3,3,128,128]{3,2,1,0:T(8,128)(2,1)} %param.16) | copy-start | bytes 884740
  13.5 15.4 %collective-permute-start.5 = (bf16[12,4,32]{2,0,1:T(8,128)(2,1)S(1)}, bf16[12,4,32]{2,0,1:T(8,128)(2,1)S(1)}, u32[]{:S(2)}, u32[]{:S(2)}) collective-permute-start(bf16[12,4,32]{2,0,1:T(8,128)(2,1)S(1)} %constant_dynamic-slice_fusion), channel_id=1, source_target_pairs={{0,2},{1,3},{2,0},{3,1},{4,6},{5,7},{6,4},{7,5},{8,10},{9,11},{10,... | collective-permute-start | bytes 9224 | tf_op jit(solution)/shard_map/ppermute | solution.py:217
  17.7 15.5 %collective-permute-start.2 = (bf16[4,9,256]{2,1,0:T(8,128)(2,1)S(1)}, bf16[4,9,256]{2,1,0:T(8,128)(2,1)S(1)}, u32[]{:S(2)}, u32[]{:S(2)}) collective-permute-start(bf16[4,9,256]{2,1,0:T(8,128)(2,1)S(1)} %get-tuple-element.11), channel_id=1, source_target_pairs={{4,0},{8,4},{12,8},{16,12},{20,16},{24,20},{28,24},{5,1},{9,5},{13... | collective-permute-start | bytes 55304 | tf_op jit(solution)/shard_map/ppermute | solution.py:256
  19.0 14.0 %collective-permute-start.1 = (bf16[4,9,256]{2,1,0:T(8,128)(2,1)S(1)}, bf16[4,9,256]{2,1,0:T(8,128)(2,1)S(1)}, u32[]{:S(2)}, u32[]{:S(2)}) collective-permute-start(bf16[4,9,256]{2,1,0:T(8,128)(2,1)S(1)} %get-tuple-element.12), channel_id=1, source_target_pairs={{0,4},{4,8},{8,12},{12,16},{16,20},{20,24},{24,28},{1,5},{5,9},{9,... | collective-permute-start | bytes 55304 | tf_op jit(solution)/shard_map/ppermute | solution.py:255
  22.1 10.8 %collective-permute-start = (bf16[4,18,256]{2,1,0:T(8,128)(2,1)S(1)}, bf16[4,18,256]{2,1,0:T(8,128)(2,1)S(1)}, u32[]{:S(2)}, u32[]{:S(2)}) collective-permute-start(bf16[4,18,256]{2,1,0:T(8,128)(2,1)S(1)} %pad_maximum_fusion.1), channel_id=1, source_target_pairs={{0,2},{1,3},{2,0},{3,1},{4,6},{5,7},{6,4},{7,5},{8,10},{9,11},{10,... | collective-permute-start | bytes 110600 | tf_op jit(solution)/shard_map/ppermute | solution.py:217
  23.5 1.0 %copy-start.2 = (bf16[3,3,128,128]{3,2,1,0:T(8,128)(2,1)S(1)}, bf16[3,3,128,128]{3,2,1,0:T(8,128)(2,1)}, u32[]{:S(2)}) copy-start(bf16[3,3,128,128]{3,2,1,0:T(8,128)(2,1)} %param.17) | copy-start | bytes 884740
  24.4 1.0 %copy-start.3 = (bf16[3,3,128,128]{3,2,1,0:T(8,128)(2,1)S(1)}, bf16[3,3,128,128]{3,2,1,0:T(8,128)(2,1)}, u32[]{:S(2)}) copy-start(bf16[3,3,128,128]{3,2,1,0:T(8,128)(2,1)} %param.18) | copy-start | bytes 884740
  25.4 1.0 %copy-start.4 = (bf16[3,3,16,128]{3,2,1,0:T(8,128)(2,1)S(1)}, bf16[3,3,16,128]{3,2,1,0:T(8,128)(2,1)}, u32[]{:S(2)}) copy-start(bf16[3,3,16,128]{3,2,1,0:T(8,128)(2,1)} %param.14) | copy-start | bytes 110596
  25.4 2.9 %copy-start.5 = (bf16[3,3,128,4]{2,3,1,0:T(4,128)(2,1)S(1)}, bf16[3,3,128,4]{2,3,1,0:T(4,128)(2,1)}, u32[]{:S(2)}) copy-start(bf16[3,3,128,4]{2,3,1,0:T(4,128)(2,1)} %param.19) | copy-start | bytes 27652
  29.1 8.3 %collective-permute-start.6 = (bf16[12,8,2]{2,0,1:T(8,128)(2,1)S(1)}, bf16[12,8,2]{2,0,1:T(8,128)(2,1)S(1)}, u32[]{:S(2)}, u32[]{:S(2)}) collective-permute-start(bf16[12,8,2]{2,0,1:T(8,128)(2,1)S(1)} %get-tuple-element.15), channel_id=1, source_target_pairs={{0,1},{1,2},{2,3},{3,0},{4,5},{5,6},{6,7},{7,4},{8,9},{9,10},{10,1... | collective-permute-start | bytes 1160 | tf_op jit(solution)/shard_map/ppermute | solution.py:224
  30.7 6.6 %collective-permute-start.7 = (bf16[12,8,2]{2,0,1:T(8,128)(2,1)S(1)}, bf16[12,8,2]{2,0,1:T(8,128)(2,1)S(1)}, u32[]{:S(2)}, u32[]{:S(2)}) collective-permute-start(bf16[12,8,2]{2,0,1:T(8,128)(2,1)S(1)} %get-tuple-element.16), channel_id=1, source_target_pairs={{1,0},{2,1},{3,2},{0,3},{5,4},{6,5},{7,6},{4,7},{9,8},{10,9},{11,1... | collective-permute-start | bytes 1160 | tf_op jit(solution)/shard_map/ppermute | solution.py:225
  33.4 6.6 %collective-permute-start.3 = (bf16[4,50,16]{2,1,0:T(8,128)(2,1)S(1)}, bf16[4,50,16]{2,1,0:T(8,128)(2,1)S(1)}, u32[]{:S(2)}, u32[]{:S(2)}) collective-permute-start(bf16[4,50,16]{2,1,0:T(8,128)(2,1)S(1)} %get-tuple-element.9), channel_id=1, source_target_pairs={{0,1},{1,2},{2,3},{3,0},{4,5},{5,6},{6,7},{7,4},{8,9},{9,10},{10,1... | collective-permute-start | bytes 19208 | tf_op jit(solution)/shard_map/ppermute | solution.py:224
  33.5 6.6 %collective-permute-start.4 = (bf16[4,50,16]{2,1,0:T(8,128)(2,1)S(1)}, bf16[4,50,16]{2,1,0:T(8,128)(2,1)S(1)}, u32[]{:S(2)}, u32[]{:S(2)}) collective-permute-start(bf16[4,50,16]{2,1,0:T(8,128)(2,1)S(1)} %get-tuple-element.10), channel_id=1, source_target_pairs={{1,0},{2,1},{3,2},{0,3},{5,4},{6,5},{7,6},{4,7},{9,8},{10,9},{11,1... | collective-permute-start | bytes 19208 | tf_op jit(solution)/shard_map/ppermute | solution.py:225
where the time goes:
time: 86.6 us; the launch traced here: 86.3 us
  Pallas kernels  45.1 us (52%)
  starting transfers between devices  15.1 us (17%)
  blocking collectives  10.7 us (12%)
  other arithmetic  7.2 us (8%)
  local copies, waits for them, and re-layouts  4.1 us (5%)
  between operations  2.08 us (2%)
  waiting for transfers between devices  2.03 us (2%)
    pallas_call x1, Pallas kernels, body(): pl.pallas_call(call, out_shape=jax.ShapeDtypeStruct(current_sample.shape,...  45.1 us
    all_gather x1, blocking collectives, body(): lax.all_gather(coarse_fields.astype(bf16), 'lat', axis=1, tiled=True)  10.7 us
    ppermute x2, starting transfers between devices, columns_with_halo(): after = lax.ppermute(own[:, :, :halo], 'lon', [(j, i) for i, j in up])  6.09 us
    concatenate x5, other arithmetic, pair_weights(): both = jnp.concatenate([low, high], axis=3)  4.46 us
    ppermute x1, starting transfers between devices, body(): above = lax.ppermute(noisy[:, -ROW_HALO:], 'lat', up)  3.03 us
    ppermute x2, starting transfers between devices, across_pole(): lax.ppermute(edges, 'lon', [(i, (i + sectors // 2) % sectors) for i in ra...  2.99 us
    ppermute x2, waiting for transfers between devices, columns_with_halo(): before = lax.ppermute(own[:, :, -halo:], 'lon', up)  2.01 us
  transfers between devices with their start and end apart: 8, of which 1 were waited for; matrix products, arithmetic and copies ran while one was open for 9% of the time, Pallas kernels for 0%

commit v1 on v0

--- a/solution.py
+++ b/solution.py
@@ -203,27 +203,149 @@
     return both.reshape(-1, both.shape[3])
 
 
-def rows_with_halo(own, above, below, across_first, across_last):
-    band = lax.axis_index("lat")
-    bands = lax.axis_size("lat")
-    north = jnp.where(band == 0, jnp.flip(across_first, 1), above)
-    south = jnp.where(band == bands - 1, jnp.flip(across_last, 1), below)
-    return jnp.concatenate([north, own, south], axis=1)
-
-
-def across_pole(own, halo):
-    sectors = lax.axis_size("lon")
-    edges = jnp.concatenate([own[:, :halo], own[:, -halo:]], axis=1)
-    got = lax.ppermute(edges, "lon", [(i, (i + sectors // 2) % sectors) for i in range(sectors)])
-    return got[:, :halo], got[:, halo:]
-
-
-def columns_with_halo(own, halo):
-    sectors = lax.axis_size("lon")
-    up = [(i, (i + 1) % sectors) for i in range(sectors)]
-    before = lax.ppermute(own[:, :, -halo:], "lon", up)
-    after = lax.ppermute(own[:, :, :halo], "lon", [(j, i) for i, j in up])
-    return jnp.concatenate([before, own, after], axis=2)
+MESH = pl.DeviceIdType.MESH
+LANE = 128
+SENT_ROWS = 12
+
+
+def sector_offsets(sectors):
+    half = sectors // 2
+    found = []
+    for off in (0, 1, -1, half, half + 1, half - 1):
+        if off % sectors not in found:
+            found.append(off % sectors)
+    return found
+
+
+def exchange_kernel(
+    bands, sectors, noisy_ref, tile_ref, ext_ref, tiles_ref, edge, side, tiles, edge_send, edge_recv, side_send,
+    side_recv, tile_send, tile_recv,
+):
+    band, sector = lax.axis_index("lat"), lax.axis_index("lon")
+    offsets = sector_offsets(sectors)
+    count = len(offsets)
+    own_rows, width = noisy_ref.shape
+    sent = edge.shape[1]
+    others = [(d, k) for d in range(bands) for k in range(count) if d or offsets[k]]
+
+    def peer(d, k):
+        return lax.rem(band + d, bands), lax.rem(sector + sectors - offsets[k], sectors)
+
+    barrier = pltpu.get_barrier_semaphore()
+    for d, k in others:
+        pl.semaphore_signal(barrier, inc=1, device_id=peer(d, k), device_id_type=MESH)
+    pl.semaphore_wait(barrier, len(others))
+
+    places = (
+        (pl.ds(LANE + width, LANE), pl.ds(0, LANE)),
+        (pl.ds(LANE, width), pl.ds(0, width)),
+        (pl.ds(0, LANE), pl.ds(width - LANE, LANE)),
+    )
+    started = []
+    arriving = []
+    for d, k in others:
+        n = d * count + k
+        copy = pltpu.make_async_remote_copy(
+            src_ref=tile_ref,
+            dst_ref=tiles.at[n],
+            send_sem=tile_send.at[n],
+            recv_sem=tile_recv.at[n],
+            device_id=peer(d, k),
+            device_id_type=MESH,
+        )
+        copy.start()
+        started.append(copy)
+        arriving.append(copy)
+    for way, start in enumerate((0, own_rows - sent)):
+        polar = band == (0 if way == 0 else bands - 1)
+        part = jnp.where(polar, way, 1 - way)
+        to_band = jnp.where(polar, band, band + (2 * way - 1))
+        turn = jnp.where(polar, sectors // 2, 0)
+        for c, (there, here) in enumerate(places):
+            target = (to_band, lax.rem(sector + sectors + (c - 1) + turn, sectors))
+            copy = pltpu.make_async_remote_copy(
+                src_ref=noisy_ref.at[pl.ds(start, sent), here],
+                dst_ref=edge.at[part, :, there],
+                send_sem=edge_send.at[way, c],
+                recv_sem=edge_recv.at[part, c],
+                device_id=target,
+                device_id_type=MESH,
+            )
+            copy.start()
+            started.append(copy)
+            arriving.append(
+                pltpu.make_async_remote_copy(
+                    src_ref=noisy_ref.at[pl.ds(start, sent), here],
+                    dst_ref=edge.at[way, :, there],
+                    send_sem=edge_send.at[way, c],
+                    recv_sem=edge_recv.at[way, c],
+                    device_id=target,
+                    device_id_type=MESH,
+                )
+            )
+    for c in (0, 2):
+        copy = pltpu.make_async_remote_copy(
+            src_ref=noisy_ref.at[:, places[c][1]],
+            dst_ref=side.at[1 - c // 2],
+            send_sem=side_send.at[c // 2],
+            recv_sem=side_recv.at[1 - c // 2],
+            device_id=(band, lax.rem(sector + sectors + (c - 1), sectors)),
+            device_id_type=MESH,
+        )
+        copy.start()
+        started.append(copy)
+        arriving.append(copy)
+    ext_ref[pl.ds(sent, own_rows), pl.ds(LANE, width)] = noisy_ref[...]
+    for copy in arriving:
+        copy.wait_recv()
+    for copy in started:
+        copy.wait_send()
+    ext_ref[pl.ds(sent, own_rows), pl.ds(0, LANE)] = side[0]
+    ext_ref[pl.ds(sent, own_rows), pl.ds(LANE + width, LANE)] = side[1]
+    ext_ref[pl.ds(0, sent), :] = edge[0]
+    ext_ref[pl.ds(sent + own_rows, sent), :] = edge[1]
+    for d in range(bands):
+        for k in range(count):
+            from_band = lax.rem(band + bands - d, bands)
+            tiles_ref[from_band, k] = tiles[d * count + k] if d or offsets[k] else tile_ref[...]
+
+
+def exchange(noisy, tile):
+    bands, sectors = lax.axis_size("lat"), lax.axis_size("lon")
+    count = len(sector_offsets(sectors))
+    variables, rows, width = noisy.shape
+    noisy = noisy.transpose(1, 0, 2).reshape(rows * variables, width)
+    sent = SENT_ROWS * variables
+    wide = width + 2 * LANE
+    vmem = pl.BlockSpec(memory_space=pltpu.VMEM)
+    dma = pltpu.SemaphoreType.DMA
+
+    def call(*refs):
+        exchange_kernel(bands, sectors, *refs)
+
+    ext, tiles = pl.pallas_call(
+        call,
+        out_shape=(
+            jax.ShapeDtypeStruct((rows * variables + 2 * sent, wide), bf16),
+            jax.ShapeDtypeStruct((bands, count) + tile.shape, bf16),
+        ),
+        in_specs=[vmem] * 2,
+        out_specs=[vmem] * 2,
+        scratch_shapes=[
+            pltpu.VMEM((2, sent, wide), bf16),
+            pltpu.VMEM((2, rows * variables, LANE), bf16),
+            pltpu.VMEM((bands * count,) + tile.shape, bf16),
+            dma((2, 3)),
+            dma((2, 3)),
+            dma((2,)),
+            dma((2,)),
+            dma((bands * count,)),
+            dma((bands * count,)),
+        ],
+        compiler_params=pltpu.CompilerParams(collective_id=0, has_side_effects=True),
+    )(noisy, tile)
+    ext = ext.reshape(rows + 2 * SENT_ROWS, variables, wide)
+    return ext[:, :, LANE - COL_HALO : LANE + width + COL_HALO], tiles
 
 
 def body(
@@ -250,29 +372,41 @@
     perturbed = current_sample + math.sqrt(sigma_hat**2 - sigma_now**2) * churn_noise
     scale_in = 1.0 / math.sqrt(sigma_hat**2 + sigma_data**2)
     noisy = (perturbed * scale_in).astype(bf16)
-    up = [(i, i + 1) for i in range(bands - 1)]
-    down = [(j, i) for i, j in up]
-    above = lax.ppermute(noisy[:, -ROW_HALO:], "lat", up)
-    below = lax.ppermute(noisy[:, :ROW_HALO], "lat", down)
-    ext = columns_with_halo(rows_with_halo(noisy, above, below, *across_pole(noisy, ROW_HALO)), COL_HALO)
-
-    block_rows = coarse_fields.shape[1]
-    gathered = lax.all_gather(coarse_fields.astype(bf16), "lat", axis=1, tiled=True)
-
-    def tile(which):
+    block_rows, block_cols = coarse_fields.shape[1:]
+    packed = coarse_fields.astype(bf16).reshape(coarse_fields.shape[0], -1)
+    packed = jnp.pad(packed, ((variables, ins - variables - packed.shape[0]), (0, 0)))
+    got, tiles = exchange(noisy, packed)
+
+    own = got[SENT_ROWS : SENT_ROWS + rows]
+    first, last = got[:SENT_ROWS], got[SENT_ROWS + rows :]
+    at_north, at_south = band == 0, band == bands - 1
+    above = jnp.where(at_north, jnp.flip(first[:ROW_HALO], 0), first[-ROW_HALO:])
+    below = jnp.where(at_south, jnp.flip(last[-ROW_HALO:], 0), last[:ROW_HALO])
+    ext = jnp.concatenate([above, own, below], axis=0)
+    ext = jnp.pad(ext, ((0, 0), (0, ins - variables), (0, 0))).reshape(ext_rows * ins, -1)
+
+    sectors = lax.axis_size("lon")
+    offsets = sector_offsets(sectors)
+    side_cols = COL_HALO // RATIO
+
+    def block(which, middle):
         slot = tile_owner[jnp.clip(which, 0, bands - 1)]
-        return lax.dynamic_slice_in_dim(gathered, slot * block_rows, block_rows, 1)
-
-    own = tile(band)
-    cells = rows_with_halo(
-        own, tile(band - 1)[:, -CELL_HALO:], tile(band + 1)[:, :CELL_HALO], *across_pole(own, CELL_HALO)
-    )
-    cells = columns_with_halo(cells, COL_HALO // RATIO)
-
-    ext = jnp.pad(ext.transpose(1, 0, 2), ((0, 0), (0, ins - variables), (0, 0))).reshape(ext_rows * ins, -1)
-    cells = cells.transpose(1, 0, 2)
-    cells = jnp.pad(cells, ((0, 0), (variables, 0), (0, 128 - cells.shape[2])))
-    cells = cells.reshape(-1, 128)
+        all_sectors = lax.dynamic_index_in_dim(tiles, slot, 0, False)
+
+        def at(off):
+            return all_sectors[offsets.index(off % sectors)].reshape(ins, block_rows, block_cols)
+
+        return jnp.concatenate(
+            [at(middle - 1)[:, :, -side_cols:], at(middle), at(middle + 1)[:, :, :side_cols]], axis=2
+        )
+
+    half = sectors // 2
+    centre = block(band, 0)
+    opposite = block(band, half)
+    upper = jnp.where(at_north, jnp.flip(opposite[:, :CELL_HALO], 1), block(band - 1, 0)[:, -CELL_HALO:])
+    lower = jnp.where(at_south, jnp.flip(opposite[:, -CELL_HALO:], 1), block(band + 1, 0)[:, :CELL_HALO])
+    cells = jnp.concatenate([upper, centre, lower], axis=1).transpose(1, 0, 2)
+    cells = jnp.pad(cells, ((0, 0), (0, 0), (0, 128 - cells.shape[2]))).reshape(-1, 128)
     out_w = jnp.pad(jnp.transpose(output_kernel, (0, 1, 3, 2)), ((0, 0), (0, 0), (0, 8 - variables), (0, 0)))
     out_w = out_w.reshape(-1, channels)
 

time: 86.6 us -> 84.2 us (0.972)
  Pallas kernels: 45.1 us -> 61 us
  starting transfers between devices: 15.1 us -> 0 us
  blocking collectives: 10.7 us -> 0 us
  local copies, waits for them, and re-layouts: 4.1 us -> 7.98 us
  between operations: 2.08 us -> 5.65 us
  waiting for transfers between devices: 2.03 us -> 0 us
  other arithmetic: 7.2 us -> 9.04 us
    pallas_call x0 -> x1, Pallas kernels: none -> 15.9 us  [exchange(): pl.pallas_call(call, out_shape=(jax.ShapeDtypeStruct((rows * variables +...]
    ppermute x8 -> x0, starting transfers between devices: 15.1 us -> none  [the longest x2 6.09 us: columns_with_halo(): after = lax.ppermute(own[:, :, :halo], 'lon', [(j, i) for i, j in up])]
    all_gather x1 -> x0, blocking collectives: 10.7 us -> none  [body(): lax.all_gather(coarse_fields.astype(bf16), 'lat', axis=1, tiled=True)]
    ppermute x8 -> x0, waiting for transfers between devices: 2.03 us -> none  [the longest x2 2.01 us: columns_with_halo(): before = lax.ppermute(own[:, :, -halo:], 'lon', up)]
    reshape x0 -> x3, local copies, waits for them, and re-layouts: none -> 1.74 us  [the longest x1 1 us: exchange(): ext = ext.reshape(rows + 2 * SENT_ROWS, variables, wide)]
    convert_element_type x2 -> x1, other arithmetic: 2.39 us -> 0.75 us  [body(): packed = coarse_fields.astype(bf16).reshape(coarse_fields.shape[0], -1)]
    transpose x2, other arithmetic: 0.25 us -> 1.73 us  [the longest x1 1.64 us: exchange(): noisy = noisy.transpose(1, 0, 2).reshape(rows * variables, width)]
    slice x5 -> x8, local copies, waits for them, and re-layouts: 0.19 us -> 1.34 us  [the longest x1 0.79 us: at(): all_sectors[offsets.index(off % sectors)]]
  transfers between devices with their start and end apart: 8 -> 0, of which waited for: 1 -> 0; matrix products, arithmetic and copies ran while one was open for 9% -> 0% of each run, Pallas kernels for 0% -> 0%
where the time goes in v1:
time: 84.2 us; the launch traced here: 83.7 us
  Pallas kernels  61 us (72%)
  other arithmetic  9.04 us (11%)
  local copies, waits for them, and re-layouts  7.98 us (9%)
  between operations  5.65 us (7%)
    pallas_call x1, Pallas kernels, body(): pl.pallas_call(call, out_shape=jax.ShapeDtypeStruct(current_sample.shape,...  45.1 us
    pallas_call x1, Pallas kernels, exchange(): pl.pallas_call(call, out_shape=(jax.ShapeDtypeStruct((rows * variables +...  15.9 us
    concatenate x5, other arithmetic, pair_weights(): both = jnp.concatenate([low, high], axis=3)  5.33 us

profile of v1, /device:TPU:0, one launch (start us, length us, event | category | flops | bytes accessed | tf_op | source)
XLA Modules:
  0.0 83.7 jit_solution(5293481179589295611)
XLA Ops:
  0.0 1.4 %fusion.27 = (s32[1]{0:T(128)}, s32[1]{0:T(128)}, s32[1]{0:T(128)}) fusion(s32[8]{0:T(128)} %param.13, s32[]{:T(128)S(6)} %min.12, s32[]{:T(128)S(6)} %min.11, s32[]{:T(128)S(6)} %min.13), kind=kLoop, calls=%fused_computation.52 | loop fusion | bytes 36 | tf_op jit(solution)/shard_map/dynamic_slice | solution.py:393
  6.9 0.7 convert_element_type.29
  7.7 0.1 reshape.54
  7.7 0.6 pad.50.refs_1_
  8.3 1.3 %pad.63 = bf16[3,3,8,128]{3,2,1,0:T(8,128)(2,1)} pad(bf16[3,3,4,128]{3,2,1,0:T(4,128)(2,1)} %bitcast.48, bf16[]{:T(256)} %constant.30.clone.1), padding=0_0x0_0x0_4x0_0 | pad | bytes 27650 | tf_op jit(solution)/shard_map/jit(_pad)/pad | solution.py:410
  9.7 1.5 %fusion.19 = bf16[4,3,16,256]{3,2,1,0:T(8,128)(2,1)} fusion(bf16[3,3,16,128]{3,2,1,0:T(8,128)(2,1)} %param.14), kind=kLoop, calls=%fused_computation.26 | loop fusion | flops 393216 | bytes 135168 | tf_op jit(solution)/shard_map/concatenate | solution.py:202
  11.1 1.6 %fusion.20 = (bf16[32,4,256]{2,0,1:T(8,128)(2,1)S(1)}, f32[4,32,256]{2,1,0:T(8,128)}) fusion(f32[4,32,256]{2,1,0:T(8,128)} %param.10, f32[4,32,256]{2,1,0:T(8,128)} %param.11), kind=kLoop, calls=%fused_computation.27 | loop fusion | flops 131072 | bytes 458752 | tf_op jit(solution)/shard_map/transpose | solution.py:317
  12.8 0.1 copy.23
  12.8 0.7 reshape.53.refs_0_
  13.5 15.9 %shard_map.100 = (bf16[224,512]{1,0:T(8,128)(2,1)}, bf16[8,4,16,128]{3,2,1,0:T(8,128)(2,1)}) custom-call(bf16[128,256]{1,0:T(8,128)(2,1)} %reshape.53.refs_0_, bf16[16,128]{1,0:T(8,128)(2,1)} %pad.50.refs_1_), custom_call_target="tpu_custom_call" | custom-call | tf_op jit(solution)/shard_map/pallas_call | solution.py:326
  29.4 1.0 %reshape.55 = bf16[56,4,512]{2,1,0:T(4,128)(2,1)S(1)} reshape(bf16[224,512]{1,0:T(8,128)(2,1)} %get-tuple-element.7) | data formatting | bytes 458752 | tf_op jit(solution)/shard_map/reshape | solution.py:347
  30.4 0.8 constant_dynamic-slice_fusion.2
  31.2 0.1 reshape_squeeze.35
  31.3 0.1 slice.138
  31.4 0.1 reshape_squeeze.40
  31.4 0.1 reshape_squeeze.39
  31.5 0.1 slice.143
  31.6 0.1 reshape_squeeze.36
  31.7 0.1 reshape_squeeze.34
  31.8 0.1 reshape_squeeze.33
  31.9 0.1 reshape_squeeze.32
  32.0 0.1 reshape_squeeze.41
  32.1 0.1 reshape_squeeze.37
  32.2 0.1 reshape_squeeze.38
  32.2 0.1 fusion.26
  32.4 0.1 fusion.25
  32.5 0.1 pad_maximum_fusion
  32.6 0.0 copy-start
  32.6 0.1 fusion.21
  32.7 0.1 maximum_bitcast_fusion
  32.8 0.6 pad.52
  33.4 0.1 fusion.23
  33.5 0.1 slice_select_fusion.1
  33.6 0.1 slice.132
  33.7 0.0 copy-start.1
  33.7 1.0 %fusion.16 = bf16[50,16,288]{2,1,0:T(8,128)(2,1)} fusion(bf16[9,4,288]{2,1,0:T(4,128)(2,1)S(1)} %get-tuple-element.12, bf16[32,4,288]{2,1,0:T(4,128)(2,1)S(1)} %slice.132, bf16[9,4,288]{2,1,0:T(4,128)(2,1)S(1)} %get-tuple-element.11), kind=kLoop, calls=%fused_computation.19 | loop fusion | flops 2304000 | bytes 576000 | tf_op jit(solution)/shard_map/concatenate | solution.py:385
  34.7 0.0 copy-done
  34.7 1.0 %fusion.11 = bf16[4,3,128,256]{3,2,1,0:T(8,128)(2,1)} fusion(bf16[3,3,128,128]{3,2,1,0:T(8,128)(2,1)S(1)} %copy-done), kind=kLoop, calls=%fused_computation.14 | loop fusion | flops 3145728 | bytes 1081344 | tf_op jit(solution)/shard_map/concatenate | solution.py:202
  35.7 0.0 copy-start.2
  35.7 0.0 copy-done.1
  35.7 1.0 %fusion.12 = bf16[4,3,128,256]{3,2,1,0:T(8,128)(2,1)} fusion(bf16[3,3,128,128]{3,2,1,0:T(8,128)(2,1)S(1)} %copy-done.1), kind=kLoop, calls=%fused_computation.15 | loop fusion | flops 3145728 | bytes 1081344 | tf_op jit(solution)/shard_map/concatenate | solution.py:202
  36.7 0.0 copy-start.3
  36.7 0.0 copy-done.2
  36.7 0.9 %fusion.13 = bf16[4,3,128,256]{3,2,1,0:T(8,128)(2,1)} fusion(bf16[3,3,128,128]{3,2,1,0:T(8,128)(2,1)S(1)} %copy-done.2), kind=kLoop, calls=%fused_computation.16 | loop fusion | flops 3145728 | bytes 1081344 | tf_op jit(solution)/shard_map/concatenate | solution.py:202
  37.6 0.0 copy-done.3
  37.6 1.0 %fusion.14 = bf16[4,3,128,256]{3,2,1,0:T(8,128)(2,1)} fusion(bf16[3,3,128,128]{3,2,1,0:T(8,128)(2,1)S(1)} %copy-done.3), kind=kLoop, calls=%fused_computation.17 | loop fusion | flops 3145728 | bytes 1081344 | tf_op jit(solution)/shard_map/concatenate | solution.py:202
  38.6 45.1 %shard_map.101 = f32[4,32,256]{2,1,0:T(8,128)} custom-call(bf16[800,288]{1,0:T(8,128)(2,1)} %bitcast.42, bf16[128,128]{1,0:T(8,128)(2,1)} %bitcast.44, f32[4,32,256]{2,1,0:T(8,128)} %get-tuple-element.10.refs_2_, bf16[192,256]{1,0:T(8,128)(2,1)} %bitcast.43, bf16[1536,256]{1,0:T(8,128)(2,1)} %bitcast.38, bf16[1536,256]{1,0:T(8,128)(2,1)} %bitcast.39, ...), custom_call_target="tpu_custom_call" | custom-call | tf_op jit(solution)/shard_map/pallas_call | solution.py:422
  (13 shorter events, 0.1 us)
Async XLA Ops:
  32.6 2.1 %copy-start = (bf16[3,3,128,128]{3,2,1,0:T(8,128)(2,1)S(1)}, bf16[3,3,128,128]{3,2,1,0:T(8,128)(2,1)}, u32[]{:S(2)}) copy-start(bf16[3,3,128,128]{3,2,1,0:T(8,128)(2,1)} %param.15) | copy-start | bytes 884740
  33.7 2.0 %copy-start.1 = (bf16[3,3,128,128]{3,2,1,0:T(8,128)(2,1)S(1)}, bf16[3,3,128,128]{3,2,1,0:T(8,128)(2,1)}, u32[]{:S(2)}) copy-start(bf16[3,3,128,128]{3,2,1,0:T(8,128)(2,1)} %param.16) | copy-start | bytes 884740
  35.7 1.0 %copy-start.2 = (bf16[3,3,128,128]{3,2,1,0:T(8,128)(2,1)S(1)}, bf16[3,3,128,128]{3,2,1,0:T(8,128)(2,1)}, u32[]{:S(2)}) copy-start(bf16[3,3,128,128]{3,2,1,0:T(8,128)(2,1)} %param.17) | copy-start | bytes 884740
  36.7 1.0 %copy-start.3 = (bf16[3,3,128,128]{3,2,1,0:T(8,128)(2,1)S(1)}, bf16[3,3,128,128]{3,2,1,0:T(8,128)(2,1)}, u32[]{:S(2)}) copy-start(bf16[3,3,128,128]{3,2,1,0:T(8,128)(2,1)} %param.18) | copy-start | bytes 884740

commit v2 on v1

--- a/solution.py
+++ b/solution.py
@@ -48,34 +48,97 @@
 
 
 def kernel(
-    north, south, halves_ref, ext_ref, cell_ref, pert_ref, stem_w, first_w, second_w, cfirst_w, csecond_w, out_w,
-    res_ref, net, stem, act, hidden, fine, pooled, cact, chidden, cout, terms, rows_out,
+    band, bands, sectors, cell_shape, owner_ref, ext_ref, tiles_ref, pert_ref, stem_k, first_k, second_k, cfirst_k,
+    csecond_k, out_k, res_ref, stem_w, first_w, second_w, cfirst_w, csecond_w, net, stem, act, hidden, fine, pooled, cact, chidden, cout, terms, rows_out,
 ):
-    del halves_ref
+    north, south = band == 0, band == bands - 1
     variables, rows, width = pert_ref.shape
     channels = stem.shape[-1]
     span = stem.shape[1]
     half_span = span // 2
     pixels = span * Q
     lanes = net.shape[-1]
-    ext_cols = ext_ref.shape[1]
+    ext_cols = width + 2 * COL_HALO
     ext_rows = rows + 2 * ROW_HALO
-
-    def onehot(depth, cell):
-        at = lax.broadcasted_iota(jnp.int32, (depth, lanes), 0)
+    block_rows, block_cols = cell_shape
+
+    def onehot(depth, source, cell):
+        at = source(lax.broadcasted_iota(jnp.int32, (depth, lanes), 0))
         lane = lax.broadcasted_iota(jnp.int32, (depth, lanes), 1)
         column = (lane % Q) * span + lane // Q - 1
         inside = (column >= 0) & (column < ext_cols) & (lane < (span + 2) * Q)
         return jnp.where(inside & (at == column // cell), 1.0, 0.0).astype(bf16)
 
-    fine_cols = jnp.dot(ext_ref[...], onehot(ext_cols, 1), preferred_element_type=f32)
-    cell_cols = jnp.dot(cell_ref[...], onehot(cell_ref.shape[1], RATIO), preferred_element_type=f32)
-    for r in range(ext_rows):
-        cell = (r - ROW_HALO + CELL_HALO * RATIO) // RATIO
-        both = fine_cols[r * 16 : r * 16 + 16] + cell_cols[cell * 16 : cell * 16 + 16]
+    def cell_source(at):
+        packed = tiles_ref.shape[3]
+        place = (at // packed - 1) * block_cols + at % packed + COL_HALO // RATIO
+        return jnp.where(at % packed < block_cols, place, -1)
+
+    for taps, paired in (
+        (stem_k, stem_w),
+        (first_k, first_w),
+        (second_k, second_w),
+        (cfirst_k, cfirst_w),
+        (csecond_k, csecond_w),
+    ):
+        ins = taps.shape[2]
+        blank = jnp.zeros((ins, channels), bf16)
+        for k in range(4):
+            for b in range(3):
+                at = pl.ds((3 * k + b) * ins, ins)
+                paired[at, pl.ds(0, channels)] = taps[k, b] if k < 3 else blank
+                paired[at, pl.ds(channels, channels)] = taps[k - 1, b] if k else blank
+
+    offsets = sector_offsets(sectors)
+    packed_cols = tiles_ref.shape[3]
+    cells = []
+    for j in range(block_rows + 2 * CELL_HALO):
+        r = j - CELL_HALO
+        if r < 0:
+            mirrored, source, plain_row, mirror_row = north, band - 1, block_rows + r, -1 - r
+        elif r < block_rows:
+            mirrored, source, plain_row, mirror_row = None, band, r, r
+        else:
+            mirrored, source, plain_row, mirror_row = south, band + 1, r - block_rows, 2 * block_rows - 1 - r
+        if mirrored is not None:
+            source = jnp.where(mirrored, band, source)
+        slot = owner_ref[source]
+        parts = []
+        for t in (-1, 0, 1):
+            here = offsets.index(t % sectors)
+            shift = (packed_cols - plain_row * block_cols) % packed_cols
+            if mirrored is not None:
+                here = jnp.where(mirrored, offsets.index((t + sectors // 2) % sectors), here)
+                shift = jnp.where(mirrored, (packed_cols - mirror_row * block_cols) % packed_cols, shift)
+            parts.append(pltpu.roll(tiles_ref[slot, here].astype(f32), shift, 1))
+        cells.append(jnp.concatenate(parts, axis=1).astype(bf16))
+    cells = jnp.concatenate(cells, axis=0)
+    cell_cols = jnp.dot(cells, onehot(3 * packed_cols, cell_source, RATIO), preferred_element_type=f32)
+    fine_hot = onehot(ext_ref.shape[1], lambda at: at - (LANE - COL_HALO), 1)
+    fine_cols = jnp.dot(ext_ref[...], fine_hot, preferred_element_type=f32)
+
+    def fine_row(r):
+        return fine_cols[(r + SENT_ROWS) * variables : (r + SENT_ROWS + 1) * variables]
+
+    for i in range(ext_rows):
+        r = i - ROW_HALO
+        if r < 0:
+            value = jnp.where(north, fine_row(-1 - r - SENT_ROWS), fine_row(r))
+        elif r < rows:
+            value = fine_row(r)
+        else:
+            value = jnp.where(south, fine_row(rows + SENT_ROWS - 1 - (r - rows)), fine_row(r))
+        cell = (r + CELL_HALO * RATIO) // RATIO
+        both = jnp.concatenate([value, cell_cols[cell * 16 + variables : cell * 16 + 16]], axis=0)
         for b in range(3):
             moved = both if b == 0 else pltpu.roll(both, lanes - b * Q, 1)
-            net[r, pl.ds(b * 16, 16)] = moved.astype(bf16)
+            net[i, pl.ds(b * 16, 16)] = moved.astype(bf16)
+    gap = jnp.zeros((8 - variables, channels), f32)
+    taps = out_k[...].astype(f32)
+    out_w = []
+    for t in range(9):
+        out_w += [taps[t * variables : (t + 1) * variables], gap]
+    out_w = jnp.concatenate(out_w, axis=0).astype(bf16)
 
     def regions(halo_pairs, pairs, body):
         def step(i, carry):
@@ -83,7 +146,7 @@
             body(i, jnp.logical_not(mirrored))
             return carry
 
-        lax.fori_loop(0, 2 * halo_pairs + pairs, step, 0)
+        lax.fori_loop(0, 2 * halo_pairs + pairs, step, 0, unroll=2)
 
     def order(row, forward):
         return jnp.where(forward, row, row + 1), jnp.where(forward, row + 1, row)
@@ -151,7 +214,7 @@
         after = pltpu.roll(value[0], Q - 1, 0)[None]
         value = jnp.concatenate([before, value, after], axis=0).astype(bf16)
         terms[r] = lax.dot_general(
-            out_w[...],
+            out_w,
             value.reshape((span + 2) * Q, channels),
             (((1,), (1,)), ((), ())),
             preferred_element_type=f32,
@@ -189,18 +252,6 @@
     denom = sigma_hat**2 + sigma_data**2
     denoised = sigma_data**2 / denom * perturbed + sigma_hat * sigma_data / math.sqrt(denom) * network
     res_ref[...] = perturbed + (sigma_next - sigma_hat) / sigma_hat * (perturbed - denoised)
-
-
-def entry(bands, refs):
-    band = lax.axis_index("lat")
-    kernel(band == 0, band == bands - 1, None, *refs)
-
-
-def pair_weights(taps):
-    low = jnp.pad(taps, ((0, 1), (0, 0), (0, 0), (0, 0)))
-    high = jnp.pad(taps, ((1, 0), (0, 0), (0, 0), (0, 0)))
-    both = jnp.concatenate([low, high], axis=3)
-    return both.reshape(-1, both.shape[3])
 
 
 MESH = pl.DeviceIdType.MESH
@@ -344,8 +395,7 @@
         ],
         compiler_params=pltpu.CompilerParams(collective_id=0, has_side_effects=True),
     )(noisy, tile)
-    ext = ext.reshape(rows + 2 * SENT_ROWS, variables, wide)
-    return ext[:, :, LANE - COL_HALO : LANE + width + COL_HALO], tiles
+    return ext, tiles
 
 
 def body(
@@ -360,7 +410,6 @@
     coarse_second,
     output_kernel,
 ):
-    band = lax.axis_index("lat")
     bands = lax.axis_size("lat")
     variables, rows, width = current_sample.shape
     channels = fine_first.shape[3]
@@ -375,41 +424,10 @@
     block_rows, block_cols = coarse_fields.shape[1:]
     packed = coarse_fields.astype(bf16).reshape(coarse_fields.shape[0], -1)
     packed = jnp.pad(packed, ((variables, ins - variables - packed.shape[0]), (0, 0)))
-    got, tiles = exchange(noisy, packed)
-
-    own = got[SENT_ROWS : SENT_ROWS + rows]
-    first, last = got[:SENT_ROWS], got[SENT_ROWS + rows :]
-    at_north, at_south = band == 0, band == bands - 1
-    above = jnp.where(at_north, jnp.flip(first[:ROW_HALO], 0), first[-ROW_HALO:])
-    below = jnp.where(at_south, jnp.flip(last[-ROW_HALO:], 0), last[:ROW_HALO])
-    ext = jnp.concatenate([above, own, below], axis=0)
-    ext = jnp.pad(ext, ((0, 0), (0, ins - variables), (0, 0))).reshape(ext_rows * ins, -1)
+    ext, tiles = exchange(noisy, packed)
 
     sectors = lax.axis_size("lon")
-    offsets = sector_offsets(sectors)
-    side_cols = COL_HALO // RATIO
-
-    def block(which, middle):
-        slot = tile_owner[jnp.clip(which, 0, bands - 1)]
-        all_sectors = lax.dynamic_index_in_dim(tiles, slot, 0, False)
-
-        def at(off):
-            return all_sectors[offsets.index(off % sectors)].reshape(ins, block_rows, block_cols)
-
-        return jnp.concatenate(
-            [at(middle - 1)[:, :, -side_cols:], at(middle), at(middle + 1)[:, :, :side_cols]], axis=2
-        )
-
-    half = sectors // 2
-    centre = block(band, 0)
-    opposite = block(band, half)
-    upper = jnp.where(at_north, jnp.flip(opposite[:, :CELL_HALO], 1), block(band - 1, 0)[:, -CELL_HALO:])
-    lower = jnp.where(at_south, jnp.flip(opposite[:, -CELL_HALO:], 1), block(band + 1, 0)[:, :CELL_HALO])
-    cells = jnp.concatenate([upper, centre, lower], axis=1).transpose(1, 0, 2)
-    cells = jnp.pad(cells, ((0, 0), (0, 0), (0, 128 - cells.shape[2]))).reshape(-1, 128)
-    out_w = jnp.pad(jnp.transpose(output_kernel, (0, 1, 3, 2)), ((0, 0), (0, 0), (0, 8 - variables), (0, 0)))
-    out_w = out_w.reshape(-1, channels)
-
+    out_k = jnp.transpose(output_kernel, (0, 1, 3, 2)).reshape(-1, channels)
     lanes = -(-(span + 2) * Q // 128) * 128
     half_span = span // 2
     field = lambda n, s: pltpu.VMEM((n, s, Q, channels), bf16)
@@ -417,14 +435,16 @@
     vmem = pl.BlockSpec(memory_space=pltpu.VMEM)
 
     def call(*refs):
-        entry(bands, refs)
+        kernel(lax.axis_index("lat"), bands, sectors, (block_rows, block_cols), *refs)
 
     return pl.pallas_call(
         call,
         out_shape=jax.ShapeDtypeStruct(current_sample.shape, f32),
-        in_specs=[vmem] * 9,
+        in_specs=[pl.BlockSpec(memory_space=pltpu.SMEM)] + [vmem] * 9,
         out_specs=vmem,
         scratch_shapes=[
+            pltpu.VMEM((12 * ins, 2 * channels), bf16),
+            *[pltpu.VMEM((12 * channels, 2 * channels), bf16)] * 4,
             pltpu.VMEM((ext_rows, 3 * ins, lanes), bf16),
             field(ext_rows - 2, span),
             field(ext_rows, span + 2),
@@ -434,20 +454,21 @@
             field(fine_rows // 2, half_span + 2),
             field(fine_rows // 2, half_span + 2),
             field(fine_rows // 2 - 2, half_span),
-            pltpu.VMEM((rows + 2, out_w.shape[0], (span + 2) * Q), f32),
+            pltpu.VMEM((rows + 2, 72, (span + 2) * Q), f32),
             pltpu.VMEM((rows, 8, pixels), f32),
         ],
         compiler_params=pltpu.CompilerParams(vmem_limit_bytes=56 << 20),
     )(
+        tile_owner,
         ext,
-        cells,
+        tiles,
         perturbed,
-        pair_weights(input_kernel),
-        pair_weights(fine_first),
-        pair_weights(fine_second),
-        pair_weights(coarse_first),
-        pair_weights(coarse_second),
-        out_w,
+        input_kernel,
+        fine_first,
+        fine_second,
+        coarse_first,
+        coarse_second,
+        out_k,
     )
 
 

time: 84.2 us -> 58.4 us (0.69)
  Pallas kernels: 61 us -> 53 us
  other arithmetic: 9.04 us -> 2.39 us
  between operations: 5.65 us -> 0.01 us
  local copies, waits for them, and re-layouts: 7.98 us -> 2.7 us
    pallas_call x1, Pallas kernels: 45.1 us -> 37.1 us  [body(): pl.pallas_call(call, out_shape=jax.ShapeDtypeStruct(current_sample.shape,...]
    concatenate x7 -> x0, other arithmetic: 6.38 us -> none  [the longest x5 5.33 us: pair_weights(): both = jnp.concatenate([low, high], axis=3)]
    pad x2 -> x0, local copies, waits for them, and re-layouts: 1.93 us -> none  [the longest x1 1.31 us: body(): jnp.pad(jnp.transpose(output_kernel, (0, 1, 3, 2)), ((0, 0), (0, 0), (0,...]
    dynamic_slice x1 -> x0, local copies, waits for them, and re-layouts: 1.39 us -> none  [block(): slot = tile_owner[jnp.clip(which, 0, bands - 1)]]
    slice x8 -> x0, local copies, waits for them, and re-layouts: 1.34 us -> none  [the longest x1 0.79 us: at(): all_sectors[offsets.index(off % sectors)]]
    another operation x14 -> x0, local copies, waits for them, and re-layouts: 0.85 us -> none  [at(): all_sectors[offsets.index(off % sectors)]]
where the time goes in v2:
time: 58.4 us; the launch traced here: 58.1 us
  Pallas kernels  53 us (91%)
  local copies, waits for them, and re-layouts  2.7 us (5%)
  other arithmetic  2.39 us (4%)
    pallas_call x1, Pallas kernels, body(): pl.pallas_call(call, out_shape=jax.ShapeDtypeStruct(current_sample.shape,...  37.1 us
    pallas_call x1, Pallas kernels, exchange(): pl.pallas_call(call, out_shape=(jax.ShapeDtypeStruct((rows * variables +...  15.9 us
    transpose x1, other arithmetic, exchange(): noisy = noisy.transpose(1, 0, 2).reshape(rows * variables, width)  1.65 us
    reshape x1, local copies, waits for them, and re-layouts, body(): out_k = jnp.transpose(output_kernel, (0, 1, 3, 2)).reshape(-1, channels)  1.31 us

profile of v2, /device:TPU:0, one launch (start us, length us, event | category | flops | bytes accessed | tf_op | source)
XLA Modules:
  0.0 58.1 jit_solution(14424671456559430300)
XLA Ops:
  0.0 1.3 %reshape.11.refs_9_ = bf16[36,128]{1,0:T(8,128)(2,1)} reshape(bf16[3,3,4,128]{3,2,1,0:T(4,128)(2,1)} %bitcast.3) | data formatting | bytes 18432 | tf_op jit(solution)/shard_map/reshape | solution.py:430
  1.3 0.7 %convert_element_type.9 = bf16[12,4,32]{2,1,0:T(4,128)(2,1)S(1)} convert(f32[12,4,32]{2,1,0:T(4,128)} %param.12) | non-fusion elementwise | flops 1536 | bytes 9216 | tf_op jit(solution)/shard_map/convert_element_type | solution.py:425
  2.1 0.1 reshape.10
  2.1 0.6 %pad.4.refs_1_ = bf16[16,128]{1,0:T(8,128)(2,1)} pad(bf16[12,128]{1,0:T(8,128)(2,1)S(1)} %reshape.10, bf16[]{:T(256)} %constant.6.clone.1), padding=4_0x0_0 | pad | bytes 7170 | tf_op jit(solution)/shard_map/jit(_pad)/pad | solution.py:426
  2.7 1.6 %fusion = (bf16[32,4,256]{2,0,1:T(8,128)(2,1)S(1)}, f32[4,32,256]{2,1,0:T(8,128)}) fusion(f32[4,32,256]{2,1,0:T(8,128)} %param.10, f32[4,32,256]{2,1,0:T(8,128)} %param.11), kind=kLoop, calls=%fused_computation.2 | loop fusion | flops 131072 | bytes 458752 | tf_op jit(solution)/shard_map/transpose | solution.py:368
  4.4 0.1 copy.11
  4.4 0.7 %reshape.9.refs_0_ = bf16[128,256]{1,0:T(8,128)(2,1)} reshape(bf16[32,4,256]{2,1,0:T(4,128)(2,1)S(1)} %copy.11) | data formatting | bytes 131072 | tf_op jit(solution)/shard_map/reshape | solution.py:368
  5.1 15.9 %shard_map.100 = (bf16[224,512]{1,0:T(8,128)(2,1)}, bf16[8,4,16,128]{3,2,1,0:T(8,128)(2,1)}) custom-call(bf16[128,256]{1,0:T(8,128)(2,1)} %reshape.9.refs_0_, bf16[16,128]{1,0:T(8,128)(2,1)} %pad.4.refs_1_), custom_call_target="tpu_custom_call" | custom-call | tf_op jit(solution)/shard_map/pallas_call | solution.py:377
  21.0 37.1 %shard_map.101 = f32[4,32,256]{2,1,0:T(8,128)} custom-call(s32[8]{0:T(128)} %refs_0_.1, bf16[224,512]{1,0:T(8,128)(2,1)} %get-tuple-element.7.refs_1_, bf16[8,4,16,128]{3,2,1,0:T(8,128)(2,1)} %get-tuple-element.8.refs_2_, f32[4,32,256]{2,1,0:T(8,128)} %get-tuple-element.10.refs_3_, bf16[3,3,16,128]{3,2,1,0:T(8,128)(2,1)} %refs_4_.1, ...), custom_call_target="tpu_custom_call" | custom-call | tf_op jit(solution)/shard_map/pallas_call | solution.py:440

commit v3 on v2

--- a/solution.py
+++ b/solution.py
@@ -146,7 +146,7 @@
             body(i, jnp.logical_not(mirrored))
             return carry
 
-        lax.fori_loop(0, 2 * halo_pairs + pairs, step, 0, unroll=2)
+        lax.fori_loop(0, 2 * halo_pairs + pairs, step, 0, unroll=4)
 
     def order(row, forward):
         return jnp.where(forward, row, row + 1), jnp.where(forward, row + 1, row)
@@ -221,7 +221,7 @@
         )
         return carry
 
-    lax.fori_loop(0, rows + 2, merge_step, 0)
+    lax.fori_loop(0, rows + 2, merge_step, 0, unroll=4)
 
     def gather_step(r, carry):
         total = None
@@ -234,7 +234,7 @@
         rows_out[r] = total
         return carry
 
-    lax.fori_loop(0, rows, gather_step, 0)
+    lax.fori_loop(0, rows, gather_step, 0, unroll=4)
 
     lane = lax.broadcasted_iota(jnp.int32, (pixels, width), 0)
     column = lax.broadcasted_iota(jnp.int32, (pixels, width), 1)

time: 58.4 us -> 49.5 us (0.85)
  Pallas kernels: 53 us -> 44.1 us
    pallas_call x1, Pallas kernels: 37.1 us -> 28.2 us  [body(): pl.pallas_call(call, out_shape=jax.ShapeDtypeStruct(current_sample.shape,...]
where the time goes in v3:
time: 49.5 us; the launch traced here: 49.2 us
  Pallas kernels  44.1 us (89%)
  local copies, waits for them, and re-layouts  2.7 us (5%)
  other arithmetic  2.39 us (5%)
    pallas_call x1, Pallas kernels, body(): pl.pallas_call(call, out_shape=jax.ShapeDtypeStruct(current_sample.shape,...  28.2 us
    pallas_call x1, Pallas kernels, exchange(): pl.pallas_call(call, out_shape=(jax.ShapeDtypeStruct((rows * variables +...  15.9 us
    transpose x1, other arithmetic, exchange(): noisy = noisy.transpose(1, 0, 2).reshape(rows * variables, width)  1.65 us
    reshape x1, local copies, waits for them, and re-layouts, body(): out_k = jnp.transpose(output_kernel, (0, 1, 3, 2)).reshape(-1, channels)  1.31 us

profile of v3, /device:TPU:0, one launch (start us, length us, event | category | flops | bytes accessed | tf_op | source)
XLA Modules:
  0.0 49.2 jit_solution(11078560172579356656)
XLA Ops:
  0.0 1.3 %reshape.11.refs_9_ = bf16[36,128]{1,0:T(8,128)(2,1)} reshape(bf16[3,3,4,128]{3,2,1,0:T(4,128)(2,1)} %bitcast.3) | data formatting | bytes 18432 | tf_op jit(solution)/shard_map/reshape | solution.py:430
  1.3 0.7 %convert_element_type.9 = bf16[12,4,32]{2,1,0:T(4,128)(2,1)S(1)} convert(f32[12,4,32]{2,1,0:T(4,128)} %param.12) | non-fusion elementwise | flops 1536 | bytes 9216 | tf_op jit(solution)/shard_map/convert_element_type | solution.py:425
  2.1 0.1 reshape.10
  2.1 0.6 %pad.4.refs_1_ = bf16[16,128]{1,0:T(8,128)(2,1)} pad(bf16[12,128]{1,0:T(8,128)(2,1)S(1)} %reshape.10, bf16[]{:T(256)} %constant.6.clone.1), padding=4_0x0_0 | pad | bytes 7170 | tf_op jit(solution)/shard_map/jit(_pad)/pad | solution.py:426
  2.7 1.6 %fusion = (bf16[32,4,256]{2,0,1:T(8,128)(2,1)S(1)}, f32[4,32,256]{2,1,0:T(8,128)}) fusion(f32[4,32,256]{2,1,0:T(8,128)} %param.10, f32[4,32,256]{2,1,0:T(8,128)} %param.11), kind=kLoop, calls=%fused_computation.2 | loop fusion | flops 131072 | bytes 458752 | tf_op jit(solution)/shard_map/transpose | solution.py:368
  4.4 0.1 copy.11
  4.4 0.7 %reshape.9.refs_0_ = bf16[128,256]{1,0:T(8,128)(2,1)} reshape(bf16[32,4,256]{2,1,0:T(4,128)(2,1)S(1)} %copy.11) | data formatting | bytes 131072 | tf_op jit(solution)/shard_map/reshape | solution.py:368
  5.1 15.9 %shard_map.100 = (bf16[224,512]{1,0:T(8,128)(2,1)}, bf16[8,4,16,128]{3,2,1,0:T(8,128)(2,1)}) custom-call(bf16[128,256]{1,0:T(8,128)(2,1)} %reshape.9.refs_0_, bf16[16,128]{1,0:T(8,128)(2,1)} %pad.4.refs_1_), custom_call_target="tpu_custom_call" | custom-call | tf_op jit(solution)/shard_map/pallas_call | solution.py:377
  21.0 28.2 %shard_map.101 = f32[4,32,256]{2,1,0:T(8,128)} custom-call(s32[8]{0:T(128)} %refs_0_.1, bf16[224,512]{1,0:T(8,128)(2,1)} %get-tuple-element.7.refs_1_, bf16[8,4,16,128]{3,2,1,0:T(8,128)(2,1)} %get-tuple-element.8.refs_2_, f32[4,32,256]{2,1,0:T(8,128)} %get-tuple-element.10.refs_3_, bf16[3,3,16,128]{3,2,1,0:T(8,128)(2,1)} %refs_4_.1, ...), custom_call_target="tpu_custom_call" | custom-call | tf_op jit(solution)/shard_map/pallas_call | solution.py:440
